TPU v7x, 32 devices: a whole 2x2x4 slice. The times are simulated.
32 devices in a mesh: groups: 2 (over y), attn: 4 (over z), expert: 2 (over x), tp: 2 (over core).
Axes of the slice: x: 2, y: 2, z: 4, core: 2. Of those that a mesh axis runs over, the one named last changes fastest.
Arguments:
- residual: bfloat16 [128, 3072], P(('groups', 'attn', 'expert', 'tp')), parts along dimension 0, may hold values from -20 to 20
- queries: bfloat16 [128, 3072], P(('groups', 'attn', 'expert', 'tp')), parts along dimension 0, may hold values from -12 to 12
- new_keys: bfloat16 [128, 512], P(('groups', 'attn', 'expert', 'tp')), parts along dimension 0, may hold values from -6 to 6
- new_values: bfloat16 [128, 512], P(('groups', 'attn', 'expert', 'tp')), parts along dimension 0, may hold values from -18 to 18
- cache_keys: bfloat16 [128, 256, 512], P(('groups', 'attn', 'expert', 'tp')), parts along dimension 0, may hold values from -6 to 6
- cache_values: bfloat16 [128, 256, 512], P(('groups', 'attn', 'expert', 'tp')), parts along dimension 0, may hold values from -18 to 18
- lengths: int32 [128], P(('groups', 'attn', 'expert', 'tp')), parts along dimension 0, may hold values from 2 to 256, as said below
- norm_gain: float32 [3072], replicated, may hold values from 0.1 to 1.9
- router: bfloat16 [3072, 8], replicated, may hold values from -0.02734375 to 0.02734375
- expert_ids: int32 [128, 4], P(('groups', 'attn', 'expert', 'tp')), parts along dimension 0, may hold values from 0 to 7, all different within a row; in each aligned block of 4 rows (0 to 3, 4 to 7, ...) at most 3 rows name the same one
- w_gate: bfloat16 [8, 3072, 5376], P('expert', None, ('attn', 'tp')), may hold values from -0.109375 to 0.109375
- w_up: bfloat16 [8, 3072, 5376], P('expert', None, ('attn', 'tp')), may hold values from -0.109375 to 0.109375
- w_down: bfloat16 [8, 5376, 3072], P('expert', ('attn', 'tp')), may hold values from -0.25 to 0.25
Outputs:
- layer_out: bfloat16 [128, 3072], P(('groups', 'attn', 'expert', 'tp')), parts along dimension 0
There are 2 independent parts, one for each index of `groups`. A program takes and returns all parts, laid end to end along the dimension named above; an argument that names none is the same for every part. Nothing has to cross between parts.
Inputs may be any that keep to these rules, and one draw needn't show every extreme that they name: `expert_ids`: each row names 4 different experts. Within the rows of one device (aligned blocks of 4 rows) no expert is named more than 3 times, a bound that some block reaches. `lengths`: some request holds exactly 256 cached tokens.
All inputs are finite; a program needn't handle non-finite values.
Results may differ from a plain program's by a relative error of at most 0.01.
Values may be sent and summed in bfloat16 or wider, within the bound.
A program may use at most 128 MiB of HBM per device.

v0:
```python
import jax
import jax.numpy as jnp
from jax import lax
from jax.sharding import PartitionSpec as P

HEADS = 24
KV_HEADS = 4
HEAD_DIM = 128
EXPERTS = 8
TOPK = 4
LEN = 256
CAP = 3


norm_eps = 1e-05


def attend_local(queries, new_keys, new_values, cache_keys, cache_values, lengths):
    row_count = queries.shape[0]
    group_size = HEADS // KV_HEADS
    score_scale = HEAD_DIM ** (-0.5)
    query_heads = queries.reshape(row_count, KV_HEADS, group_size, HEAD_DIM)
    cached_keys = cache_keys.reshape(row_count, LEN, KV_HEADS, HEAD_DIM)
    cached_values = cache_values.reshape(row_count, LEN, KV_HEADS, HEAD_DIM)
    fresh_key = new_keys.reshape(row_count, KV_HEADS, HEAD_DIM)
    fresh_value = new_values.reshape(row_count, KV_HEADS, HEAD_DIM).astype(jnp.float32)
    scores = (
        jnp.einsum("rkgd,rlkd->rkgl", query_heads, cached_keys, preferred_element_type=jnp.float32)
        * score_scale
    )
    live = jnp.arange(LEN)[None, :] < lengths[:, None]
    scores = jnp.where(live[:, None, None, :], scores, -jnp.inf)
    own_score = (
        jnp.einsum("rkgd,rkd->rkg", query_heads, fresh_key, preferred_element_type=jnp.float32)
        * score_scale
    )
    highest = jnp.maximum(jnp.max(scores, axis=-1), own_score)
    weights = jnp.exp(scores - highest[..., None])
    own_weight = jnp.exp(own_score - highest)
    denominator = jnp.sum(weights, axis=-1) + own_weight
    probabilities = (weights / denominator[..., None]).astype(jnp.bfloat16)
    own_prob = (own_weight / denominator).astype(jnp.bfloat16)
    attended = jnp.einsum(
        "rkgl,rlkd->rkgd", probabilities, cached_values, preferred_element_type=jnp.float32
    )
    attended = attended + own_prob.astype(jnp.float32)[..., None] * fresh_value[:, :, None, :]
    return attended.reshape(row_count, HEADS * HEAD_DIM)


def body(
    residual,
    queries,
    new_keys,
    new_values,
    cache_keys,
    cache_values,
    lengths,
    norm_gain,
    router,
    expert_ids,
    w_gate,
    w_up,
    w_down,
):
    row_count = residual.shape[0]
    feature_count = residual.shape[1]
    expert_groups = lax.axis_size("expert")
    local_count = w_gate.shape[0]
    block_slots = local_count * CAP
    attended = attend_local(queries, new_keys, new_values, cache_keys, cache_values, lengths)
    stream = residual.astype(jnp.float32) + attended
    average = jnp.mean(stream, axis=-1, keepdims=True)
    centered = stream - average
    variance = jnp.mean(centered * centered, axis=-1, keepdims=True)
    normed = (centered * lax.rsqrt(variance + norm_eps) * norm_gain).astype(jnp.bfloat16)
    logits = jnp.dot(normed, router, preferred_element_type=jnp.float32)
    is_named = expert_ids[:, :, None] == jnp.arange(EXPERTS)[None, None, :]
    chosen = jnp.sum(jnp.where(is_named, logits[:, None, :], 0.0), axis=2)
    gate_values = jax.nn.softmax(chosen, axis=-1)
    named_counts = is_named.astype(jnp.int32).reshape(row_count * TOPK, EXPERTS)
    earlier = jnp.cumsum(named_counts, axis=0) - named_counts
    slot_index = jnp.sum(earlier * named_counts, axis=1)
    target_slot = expert_ids.reshape(-1) * CAP + slot_index
    placement = (target_slot[:, None] == jnp.arange(EXPERTS * CAP)[None, :]).reshape(
        row_count, TOPK, EXPERTS * CAP
    )
    chosen_slots = jnp.any(placement, axis=1).astype(jnp.bfloat16)
    combine = jnp.sum(jnp.where(placement, gate_values[:, :, None], 0.0), axis=1)
    outgoing = jnp.dot(chosen_slots.T, normed, preferred_element_type=jnp.float32).astype(
        jnp.bfloat16
    )
    outgoing = outgoing.reshape(expert_groups, block_slots, feature_count)
    received = lax.all_to_all(outgoing, "expert", split_axis=0, concat_axis=0, tiled=True)
    received = received.reshape(expert_groups, local_count, CAP, feature_count)
    everything = lax.all_gather(received, ("attn", "tp"), axis=0, tiled=True)
    gate_act = jnp.einsum("secd,edf->secf", everything, w_gate, preferred_element_type=jnp.float32)
    up_act = jnp.einsum("secd,edf->secf", everything, w_up, preferred_element_type=jnp.float32)
    hidden = (jax.nn.silu(gate_act) * up_act).astype(jnp.bfloat16)
    summed = lax.psum_scatter(
        jnp.einsum("secf,efd->secd", hidden, w_down, preferred_element_type=jnp.float32).astype(
            jnp.bfloat16
        ),
        ("attn", "tp"),
        scatter_dimension=0,
        tiled=True,
    )
    returned = lax.all_to_all(summed, "expert", split_axis=0, concat_axis=0, tiled=True)
    flat_out = returned.reshape(EXPERTS * CAP, feature_count).astype(jnp.float32)
    layer_out = stream + jnp.dot(combine, flat_out, precision=lax.Precision.HIGHEST)
    return layer_out.astype(jnp.bfloat16)


def solution(mesh):
    return jax.shard_map(
        body,
        mesh=mesh,
        in_specs=(
            P(("groups", "attn", "expert", "tp"), None),
            P(("groups", "attn", "expert", "tp"), None),
            P(("groups", "attn", "expert", "tp"), None),
            P(("groups", "attn", "expert", "tp"), None),
            P(("groups", "attn", "expert", "tp"), None, None),
            P(("groups", "attn", "expert", "tp"), None, None),
            P(("groups", "attn", "expert", "tp")),
            P(),
            P(),
            P(("groups", "attn", "expert", "tp"), None),
            P("expert", None, ("attn", "tp")),
            P("expert", None, ("attn", "tp")),
            P("expert", ("attn", "tp"), None),
        ),
        out_specs=P(("groups", "attn", "expert", "tp"), None),
        check_vma=False,
    )
```

profile of v0, /device:TPU:0, one launch (start us, length us, event | category | flops | bytes accessed | tf_op | source)
XLA Modules:
  0.0 153.6 jit_solution(11950329010191329404)
XLA Ops:
  6.5 0.0 copy-start
  6.5 0.0 all-gather.2.cloned.1.call-start
  6.5 0.9 reshape.123
  7.5 0.7 iota_compare_fusion.3
  8.2 0.7 reshape.138
  8.9 0.1 fusion.43
  9.0 0.0 copy-done
  9.0 0.5 fusion.42
  9.5 0.2 fusion.32
  9.7 0.0 copy-done.5
  9.8 0.3 convolution_add_fusion.1
  10.1 0.1 copy-done.2
  10.3 0.1 fusion.41
  10.4 0.2 multiply_reduce_fusion
  10.6 0.1 eq.36
  10.7 0.1 fusion.36
  10.8 0.2 select_reduce_fusion.2
  11.0 0.1 reduce_sum.67
  11.1 0.1 fusion.35
  11.2 0.0 copy-done.4
  11.2 0.1 multiply_convert_fusion
  11.3 0.2 convolution_convert_fusion
  11.6 8.8 %all_to_all.10 = bf16[2,12,3072]{2,1,0:T(8,128)(2,1)S(1)} all-to-all(bf16[2,12,3072]{2,1,0:T(8,128)(2,1)S(1)} %reshape.128), channel_id=1, replica_groups=mesh['groups'=2,'attn'=4,'expert'=2,'tp'=2] {'expert'}, dimensions={0} | all-to-all | bytes 294912 | tf_op jit(solution)/shard_map/all_to_all | solution.py:93
  20.4 0.2 copy.46
  20.6 0.7 copy.47
  21.3 0.0 all-gather.2.cloned.1.call-update
  21.3 0.0 all-reduce.3.cloned.1.call-start
  21.4 23.1 %all-gather.2.cloned.1.call-done = bf16[16,4,3,3072]{3,1,2,0:T(4,128)(2,1)} async-done(((bf16[2,4,3,3072]{3,1,2,0:T(4,128)(2,1)}), bf16[16,4,3,3072]{3,1,2,0:T(4,128)(2,1)}) %all-gather.2.cloned.1.call-update) | async-done | bytes 1179664 | tf_op jit(solution)/shard_map/all_gather | solution.py:95
  44.5 10.9 %fusion.13 = f32[16,4,3,672]{3,0,2,1:T(8,128)S(1)} fusion(bf16[4,3072,672]{1,2,0:T(8,128)(2,1)} %param.23, bf16[16,4,3,3072]{3,1,2,0:T(4,128)(2,1)} %all-gather.2.cloned.1.call-done), kind=kOutput, calls=%fused_computation.11 | convolution fusion | flops 792723456 | bytes 18210816 | tf_op jit(solution)/shard_map/secd,edf->secf/dot_general | solution.py:96
  55.4 10.5 %fusion.22 = bf16[16,4,3,672]{3,0,2,1:T(8,128)(2,1)S(1)} fusion(bf16[4,3072,672]{1,2,0:T(8,128)(2,1)} %param.24, bf16[16,4,3,3072]{3,1,2,0:T(4,128)(2,1)S(1)} %copy-done.1, f32[16,4,3,672]{3,0,2,1:T(8,128)S(1)} %fusion.13), kind=kOutput, calls=%fused_computation.14 | convolution fusion | flops 793497600 | bytes 18468864 | tf_op jit(solution)/shard_map/secd,edf->secf/dot_general | solution.py:97
  65.9 8.7 %fusion.9 = bf16[16,4,3,3072]{3,0,2,1:T(8,128)(2,1)S(1)} fusion(bf16[16,4,3,672]{3,0,2,1:T(8,128)(2,1)S(1)} %fusion.22, bf16[4,672,3072]{2,1,0:T(8,128)(2,1)} %param.25), kind=kOutput, calls=%fused_computation.7 | convolution fusion | flops 793313280 | bytes 17952768 | tf_op jit(solution)/shard_map/secf,efd->secd/dot_general | solution.py:100
  74.6 2.0 %copy.50 = bf16[16,4,3,3072]{3,1,2,0:T(4,128)(2,1)} copy(bf16[16,4,3,3072]{3,0,2,1:T(8,128)(2,1)S(1)} %fusion.9) | data formatting | bytes 2359296 | tf_op jit(solution)/shard_map/convert_element_type | solution.py:100
  76.6 0.0 all-reduce.3.cloned.1.call-update
  76.6 0.8 copy-done.7
  77.4 0.1 fusion.44
  77.5 0.2 select_reduce_fusion.1
  77.7 0.1 reduce_max.19
  77.8 0.6 dynamic-slice
  79.0 0.2 fusion.39
  79.2 0.1 fusion.38
  79.3 56.8 %all-reduce.3.cloned.1.call-done = bf16[16,4,3,3072]{3,1,2,0:T(4,128)(2,1)} async-done(((bf16[16,4,3,3072]{3,1,2,0:T(4,128)(2,1)}), bf16[16,4,3,3072]{3,1,2,0:T(4,128)(2,1)}) %all-reduce.3.cloned.1.call-update) | async-done | bytes 1179664
  136.1 1.6 %constant_dynamic-slice_fusion = bf16[2,4,3,3072]{3,1,2,0:T(4,128)(2,1)} fusion(bf16[16,4,3,3072]{3,1,2,0:T(4,128)(2,1)} %all-reduce.3.cloned.1.call-done, u32[]{:T(128)S(6)} %multiply.13), kind=kLoop, calls=%fused_computation.50 | loop fusion | bytes 294916
  137.7 3.4 %all-to-all-start.1 = ((bf16[2,4,3,3072]{3,1,2,0:T(4,128)(2,1)}), bf16[2,4,3,3072]{3,1,2,0:T(4,128)(2,1)S(1)}, u32[]{:S(2)}, u32[]{:S(2)}) async-start(bf16[2,4,3,3072]{3,1,2,0:T(4,128)(2,1)} %constant_dynamic-slice_fusion), calls=%async_computation.1 | async-start | bytes 294912 | tf_op jit(solution)/shard_map/all_to_all | solution.py:107
  141.2 0.1 select_reduce_fusion
  141.3 4.5 %all-to-all-done.1 = bf16[2,4,3,3072]{3,1,2,0:T(4,128)(2,1)S(1)} async-done(((bf16[2,4,3,3072]{3,1,2,0:T(4,128)(2,1)}), bf16[2,4,3,3072]{3,1,2,0:T(4,128)(2,1)S(1)}, u32[]{:S(2)}, u32[]{:S(2)}) %all-to-all-start.1) | async-done | bytes 147488 | tf_op jit(solution)/shard_map/all_to_all | solution.py:107
  145.7 0.1 copy.51
  145.8 0.1 reshape.130
  145.9 0.8 fusion.12
  (21 shorter events, 0.2 us)
Async XLA Ops:
  6.5 2.5 %copy-start = (bf16[4,256,512]{2,1,0:T(8,128)(2,1)S(1)}, bf16[4,256,512]{2,1,0:T(8,128)(2,1)}, u32[]{:S(2)}) copy-start(bf16[4,256,512]{2,1,0:T(8,128)(2,1)} %param.17) | copy-start | bytes 3145732
  6.5 3.2 %copy-start.5 = (bf16[4,512]{1,0:T(4,128)(2,1)S(1)}, bf16[4,512]{1,0:T(4,128)(2,1)}, u32[]{:S(2)}) copy-start(bf16[4,512]{1,0:T(4,128)(2,1)} %param.16) | copy-start | bytes 12292
  6.5 3.2 %copy-start.6 = (bf16[4,256,512]{2,1,0:T(8,128)(2,1)S(1)}, bf16[4,256,512]{2,1,0:T(8,128)(2,1)}, u32[]{:S(2)}) copy-start(bf16[4,256,512]{2,1,0:T(8,128)(2,1)} %param.18) | copy-start | bytes 3145732
  6.5 37.9 %all-gather.2.cloned.1.call-start = ((), (), s32[]{:S(2)}) async-start(), calls=%async_computation.2 | async-start | bytes 1327104 | tf_op jit(solution)/shard_map/all_gather | solution.py:95
  9.5 0.8 copy-start.2
  9.5 1.1 copy-start.3
  9.5 1.7 %copy-start.4 = (f32[3072]{0:T(1024)S(1)}, f32[3072]{0:T(1024)}, u32[]{:S(2)}) copy-start(f32[3072]{0:T(1024)} %param.20) | copy-start | bytes 36868
  21.3 114.8 %all-reduce.3.cloned.1.call-start = ((), (), s32[]{:S(2)}) async-start(), calls=%async_computation.3 | async-start | bytes 2359296
  44.5 11.0 %copy-start.1 = (bf16[16,4,3,3072]{3,1,2,0:T(4,128)(2,1)S(1)}, bf16[16,4,3,3072]{3,1,2,0:T(4,128)(2,1)}, u32[]{:S(2)}) copy-start(bf16[16,4,3,3072]{3,1,2,0:T(4,128)(2,1)} %all-gather.2.cloned.1.call-done) | copy-start | bytes 3538948
  76.6 0.8 copy-start.7
  76.6 1.2 copy-start.8
  137.7 8.0 %all-to-all-start.1 = ((bf16[2,4,3,3072]{3,1,2,0:T(4,128)(2,1)}), bf16[2,4,3,3072]{3,1,2,0:T(4,128)(2,1)S(1)}, u32[]{:S(2)}, u32[]{:S(2)}) async-start(bf16[2,4,3,3072]{3,1,2,0:T(4,128)(2,1)} %constant_dynamic-slice_fusion), calls=%async_computation.1 | async-start | bytes 294912 | tf_op jit(solution)/shard_map/all_to_all | solution.py:107
Sparse Core Ops, SparseCore 0:
  21.4 22.9 all-gather.1
  76.7 59.3 all-reduce.2
where the time goes:
time: 154 us
  waiting for transfers between devices  84.4 us (55%)
  matrix products  32.2 us (21%)
  between operations  14.2 us (9%)
  blocking collectives  8.83 us (6%)
  local copies, waits for them, and re-layouts  8.07 us (5%)
  starting transfers between devices  3.47 us (2%)
  other arithmetic  2.42 us (2%)
    unnamed x3, waiting for transfers between devices  56.8 us
    all_gather x1, waiting for transfers between devices, body(): everything = lax.all_gather(received, ('attn', 'tp'), axis=0, tiled=True)  23.1 us
    dot_general x1, matrix products, body(): jnp.einsum('secd,edf->secf', everything, w_gate, preferred_element_type=j...  10.9 us
    dot_general x1, matrix products, body(): jnp.einsum('secd,edf->secf', everything, w_up, preferred_element_type=jnp...  10.5 us
    all_to_all x1, blocking collectives, body(): lax.all_to_all(outgoing, 'expert', split_axis=0, concat_axis=0, tiled=True)  8.83 us
    dot_general x1, matrix products, body(): jnp.einsum('secf,efd->secd', hidden, w_down, preferred_element_type=jnp.f...  8.68 us
    all_to_all x1, waiting for transfers between devices, body(): lax.all_to_all(summed, 'expert', split_axis=0, concat_axis=0, tiled=True)  4.45 us
    all_to_all x1, starting transfers between devices, body(): lax.all_to_all(summed, 'expert', split_axis=0, concat_axis=0, tiled=True)  3.42 us
  transfers between devices with their start and end apart: 3, of which 3 were waited for; matrix products, arithmetic and copies ran while one was open for 1% of the time, Pallas kernels for 0%

commit v1 on v0

v1 whole, which is shorter than its diff:
```python
import functools

import jax
import jax.numpy as jnp
from jax import lax
from jax.experimental import pallas as pl
from jax.experimental.pallas import tpu as pltpu
from jax.sharding import PartitionSpec as P

HEADS = 24
KV_HEADS = 4
HEAD_DIM = 128
EXPERTS = 8
TOPK = 4
NORM_EPS = 1e-05
MESH = pl.DeviceIdType.MESH


def kernel(
    sizes,
    residual_ref,
    queries_ref,
    new_keys_ref,
    new_values_ref,
    lengths_ref,
    gain_ref,
    router_ref,
    ids_ref,
    keys_hbm,
    values_hbm,
    gate_hbm,
    up_hbm,
    down_hbm,
    out_ref,
    keys_ref,
    values_ref,
    gate_ref,
    up_ref,
    down_ref,
    query_rows,
    stream_ref,
    gathered,
    stage,
    rows_ref,
    weights_ref,
    hidden_ref,
    part_f32,
    part_b16,
    part_in,
    half_f32,
    half_b16,
    half_in,
    quad_f32,
    quad_b16,
    quad_in,
    cache_sem,
    gate_sem,
    up_sem,
    down_sem,
    ga_send,
    ga_recv,
    gx_send,
    gx_recv,
    gc_send,
    gc_recv,
    rc_send,
    rc_recv,
    rx_send,
    rx_recv,
    ra_send,
    ra_recv,
):
    n_attn, n_expert, n_tp, chunks = sizes
    a = lax.axis_index("attn")
    e = lax.axis_index("expert")
    t = lax.axis_index("tp")
    batch, width = residual_ref.shape
    local, ff, _ = gate_hbm.shape
    cache_len = keys_hbm.shape[1]
    kv_width = keys_hbm.shape[2]
    group_size = HEADS // KV_HEADS
    chunk = width // chunks
    total_rows = rows_ref.shape[0]

    cache_copies = [
        pltpu.make_async_copy(keys_hbm, keys_ref, cache_sem.at[0]),
        pltpu.make_async_copy(values_hbm, values_ref, cache_sem.at[1]),
    ]
    for copy in cache_copies:
        copy.start()

    def gate_copy(i):
        return pltpu.make_async_copy(gate_hbm.at[i], gate_ref.at[i], gate_sem.at[i])

    def up_copy(i):
        return pltpu.make_async_copy(up_hbm.at[i], up_ref.at[i], up_sem.at[i])

    def down_copy(c):
        columns = pl.ds(c * chunk, chunk)
        return pltpu.make_async_copy(
            down_hbm.at[:, :, columns], down_ref.at[c], down_sem.at[c]
        )

    for i in range(local):
        gate_copy(i).start()
        up_copy(i).start()
    for c in range(chunks):
        down_copy(c).start()

    barrier = pltpu.get_barrier_semaphore()
    partners = 0
    for axis, size, me in (("attn", n_attn, a), ("expert", n_expert, e), ("tp", n_tp, t)):
        for step in range(1, size):
            pl.semaphore_signal(
                barrier,
                inc=1,
                device_id={axis: lax.rem(me + step, size)},
                device_id_type=MESH,
            )
            partners += 1

    query_f = queries_ref[...].astype(jnp.float32)
    for r in range(batch):
        for h in range(HEADS):
            query_rows[r, h : h + 1, :] = query_f[
                r : r + 1, h * HEAD_DIM : (h + 1) * HEAD_DIM
            ]
    head_of = lax.broadcasted_iota(jnp.int32, (HEADS, kv_width), 0) // group_size
    kv_of = lax.broadcasted_iota(jnp.int32, (HEADS, kv_width), 1) // HEAD_DIM
    own_kv = head_of == kv_of
    position = lax.broadcasted_iota(jnp.int32, (HEADS, cache_len), 1)
    new_keys = new_keys_ref[...].astype(jnp.float32)
    new_values = new_values_ref[...].astype(jnp.float32)
    score_scale = HEAD_DIM ** (-0.5)
    for copy in cache_copies:
        copy.wait()
    for r in range(batch):
        query = query_rows[r]
        blocks = jnp.where(own_kv, jnp.concatenate([query] * KV_HEADS, axis=1), 0.0)
        scores = (
            lax.dot_general(
                blocks.astype(jnp.bfloat16),
                keys_ref[r],
                (((1,), (1,)), ((), ())),
                preferred_element_type=jnp.float32,
            )
            * score_scale
        )
        scores = jnp.where(position < lengths_ref[r], scores, -jnp.inf)
        own_score = (
            jnp.sum(blocks * new_keys[r : r + 1, :], axis=1, keepdims=True) * score_scale
        )
        highest = jnp.maximum(jnp.max(scores, axis=1, keepdims=True), own_score)
        weights = jnp.exp(scores - highest)
        own_weight = jnp.exp(own_score - highest)
        denominator = jnp.sum(weights, axis=1, keepdims=True) + own_weight
        probabilities = (weights / denominator).astype(jnp.bfloat16)
        own_prob = (own_weight / denominator).astype(jnp.bfloat16).astype(jnp.float32)
        mixed = jnp.dot(probabilities, values_ref[r], preferred_element_type=jnp.float32)
        mixed = jnp.where(own_kv, mixed + own_prob * new_values[r : r + 1, :], 0.0)
        attended = mixed[:, :HEAD_DIM]
        for k in range(1, KV_HEADS):
            attended = attended + mixed[:, k * HEAD_DIM : (k + 1) * HEAD_DIM]
        for h in range(HEADS):
            stream_ref[r : r + 1, h * HEAD_DIM : (h + 1) * HEAD_DIM] = attended[h : h + 1, :]

    stream = residual_ref[...].astype(jnp.float32) + stream_ref[...]
    stream_ref[...] = stream
    average = jnp.mean(stream, axis=1, keepdims=True)
    centered = stream - average
    variance = jnp.mean(centered * centered, axis=1, keepdims=True)
    normed = (centered * lax.rsqrt(variance + NORM_EPS) * gain_ref[...]).astype(jnp.bfloat16)

    logits = lax.dot_general(
        normed, router_ref[...], (((1,), (1,)), ((), ())), preferred_element_type=jnp.float32
    )
    expert_iota = lax.broadcasted_iota(jnp.int32, (batch, EXPERTS), 1)
    ids = ids_ref[...]
    named = expert_iota == ids[:, 0:1]
    for j in range(1, TOPK):
        named = named | (expert_iota == ids[:, j : j + 1])
    top = jnp.max(jnp.where(named, logits, -jnp.inf), axis=1, keepdims=True)
    raised = jnp.where(named, jnp.exp(logits - top), 0.0)
    gates = raised / jnp.sum(raised, axis=1, keepdims=True)
    gates_high = gates.astype(jnp.bfloat16)
    gates_low = (gates - gates_high.astype(jnp.float32)).astype(jnp.bfloat16)

    mine = gathered.at[t, e, a]
    mine[:, :width] = normed
    mine[:, width:] = jnp.zeros((batch, 256), jnp.bfloat16)
    mine[:, width : width + EXPERTS] = gates_high
    mine[:, width + 128 : width + 128 + EXPERTS] = gates_low

    pl.semaphore_wait(barrier, partners)

    def attn_send(step):
        return pltpu.make_async_remote_copy(
            src_ref=gathered.at[t, e, a],
            dst_ref=gathered.at[t, e, a],
            send_sem=ga_send.at[step],
            recv_sem=ga_recv.at[step],
            device_id={"attn": lax.rem(a + step, n_attn)},
            device_id_type=MESH,
        )

    def attn_arrived(step):
        source = lax.rem(a + n_attn - step, n_attn)
        block = gathered.at[t, e, source]
        return pltpu.make_async_remote_copy(
            src_ref=block,
            dst_ref=block,
            send_sem=ga_send.at[step],
            recv_sem=ga_recv.at[step],
            device_id={"attn": source},
            device_id_type=MESH,
        )

    def expert_copy(step, back, reverse):
        source_a = lax.rem(a + n_attn - back, n_attn)
        source_e = lax.rem(e + n_expert - step, n_expert) if reverse else e
        target_e = lax.rem(e + n_expert - step, n_expert) if reverse else lax.rem(e + step, n_expert)
        block = gathered.at[t, source_e, source_a]
        return pltpu.make_async_remote_copy(
            src_ref=block,
            dst_ref=block,
            send_sem=gx_send.at[step, back],
            recv_sem=gx_recv.at[step, back],
            device_id={"expert": target_e},
            device_id_type=MESH,
        )

    def core_copy(cstep, step, back, reverse):
        source_a = lax.rem(a + n_attn - back, n_attn)
        source_e = lax.rem(e + n_expert - step, n_expert)
        other = lax.rem(t + n_tp - cstep, n_tp)
        source_t = other if reverse else t
        target = other if reverse else lax.rem(t + cstep, n_tp)
        block = gathered.at[source_t, source_e, source_a]
        return pltpu.make_async_remote_copy(
            src_ref=block,
            dst_ref=block,
            send_sem=gc_send.at[cstep, step, back],
            recv_sem=gc_recv.at[cstep, step, back],
            device_id={"tp": target},
            device_id_type=MESH,
        )

    for step in range(1, n_attn):
        attn_send(step).start()

    def forward_all(back, _):
        for step in range(1, n_expert):
            expert_copy(step, back, False).start()
        for cstep in range(1, n_tp):
            core_copy(cstep, 0, back, False).start()

    forward_all(0, None)

    def arrived_then_forward(back, carry):
        attn_arrived(back).wait_recv()
        forward_all(back, None)
        return carry

    def crossed_then_forward(back, carry):
        for step in range(1, n_expert):
            expert_copy(step, back, True).wait_recv()
            for cstep in range(1, n_tp):
                core_copy(cstep, step, back, False).start()
        return carry

    def core_arrived(back, carry):
        for step in range(n_expert):
            for cstep in range(1, n_tp):
                core_copy(cstep, step, back, True).wait_recv()
        return carry

    lax.fori_loop(1, n_attn, arrived_then_forward, 0)
    lax.fori_loop(0, n_attn, crossed_then_forward, 0)
    lax.fori_loop(0, n_attn, core_arrived, 0)

    per_stage = 16 // batch
    attn_stages = n_attn // per_stage

    def assemble(i, carry):
        at_t = i // (n_expert * attn_stages)
        at_e = lax.rem(i // attn_stages, n_expert)
        at_a = lax.rem(i, attn_stages) * per_stage
        for j in range(per_stage):
            stage[j * batch : (j + 1) * batch, :] = gathered[at_t, at_e, at_a + j].astype(
                jnp.float32
            )
        at = pl.ds(pl.multiple_of(i * 16, 16), 16)
        rows_ref[at, :] = stage[:, :width].astype(jnp.bfloat16)
        weights_ref[at, :] = stage[:, width : width + 128] + stage[:, width + 128 :]
        return carry

    lax.fori_loop(0, total_rows // 16, assemble, 0)

    block_rows = min(total_rows, 64)
    row_blocks = total_rows // block_rows
    lane = lax.broadcasted_iota(jnp.int32, (block_rows, 128), 1)

    by_last = (((1,), (1,)), ((), ()))

    def first_products(i, carry):
        gate_copy(i).wait()
        up_copy(i).wait()

        def one_block(b, inner):
            at = pl.ds(pl.multiple_of(b * block_rows, block_rows), block_rows)
            gate_act = lax.dot_general(
                rows_ref[at, :], gate_ref[i], by_last, preferred_element_type=jnp.float32
            )
            up_act = lax.dot_general(
                rows_ref[at, :], up_ref[i], by_last, preferred_element_type=jnp.float32
            )
            valid = lane < EXPERTS
            chosen = jnp.where((lane == e * local + i) & valid, weights_ref[at, :], 0.0)
            scale = jnp.sum(chosen, axis=1, keepdims=True)
            hidden = gate_act / (1.0 + jnp.exp(-gate_act)) * up_act * scale
            hidden_ref[i, at, :] = hidden.astype(jnp.bfloat16)
            return inner

        lax.fori_loop(0, row_blocks, one_block, 0)
        return carry

    lax.fori_loop(0, local, first_products, 0)

    def core_sum(c, step, reverse):
        other = lax.rem(t + n_tp - step, n_tp) if reverse else lax.rem(t + step, n_tp)
        return pltpu.make_async_remote_copy(
            src_ref=part_b16.at[c, other],
            dst_ref=part_in.at[c, step],
            send_sem=rc_send.at[c, step],
            recv_sem=rc_recv.at[c, step],
            device_id={"tp": other},
            device_id_type=MESH,
        )

    def expert_sum(c, step, reverse):
        other = lax.rem(e + n_expert - step, n_expert) if reverse else lax.rem(e + step, n_expert)
        return pltpu.make_async_remote_copy(
            src_ref=half_b16.at[c, other],
            dst_ref=half_in.at[c, step],
            send_sem=rx_send.at[c, step],
            recv_sem=rx_recv.at[c, step],
            device_id={"expert": other},
            device_id_type=MESH,
        )

    def attn_sum(c, step, reverse):
        other = lax.rem(a + n_attn - step, n_attn) if reverse else lax.rem(a + step, n_attn)
        return pltpu.make_async_remote_copy(
            src_ref=quad_b16.at[c, other],
            dst_ref=quad_in.at[c, step],
            send_sem=ra_send.at[c, step],
            recv_sem=ra_recv.at[c, step],
            device_id={"attn": other},
            device_id_type=MESH,
        )

    tp_rows = total_rows // n_tp
    expert_rows = tp_rows // n_expert
    tp_block = min(tp_rows, 32)

    def compute_chunk(c):
        down_copy(c).wait()
        for at_t in range(n_tp):

            def one_block(b, inner, at_t=at_t):
                start = pl.multiple_of(b * tp_block, tp_block)
                at = pl.ds(start, tp_block)
                from_rows = pl.ds(pl.multiple_of(at_t * tp_rows + start, tp_block), tp_block)
                total = jnp.zeros((tp_block, chunk), jnp.float32)
                for i in range(local):
                    total = total + jnp.dot(
                        hidden_ref[i, from_rows, :],
                        down_ref[c, i],
                        preferred_element_type=jnp.float32,
                    )
                part_f32[at_t, at, :] = total
                part_b16[c, at_t, at, :] = total.astype(jnp.bfloat16)
                return inner

            if tp_rows > tp_block:
                lax.fori_loop(0, tp_rows // tp_block, one_block, 0)
            else:
                one_block(0, 0)
        half_f32[c] = part_f32[t].reshape(half_f32.shape[1:])
        for step in range(1, n_tp):
            core_sum(c, step, False).start()

    def compute_chunk_whole(c):
        down_copy(c).wait()
        total = jnp.dot(hidden_ref[0], down_ref[c, 0], preferred_element_type=jnp.float32)
        for i in range(1, local):
            total = total + jnp.dot(
                hidden_ref[i], down_ref[c, i], preferred_element_type=jnp.float32
            )
        for at_t in range(n_tp):
            piece = total[at_t * tp_rows : (at_t + 1) * tp_rows, :]
            part_f32[at_t] = piece
            part_b16[c, at_t] = piece.astype(jnp.bfloat16)
        half_f32[c] = part_f32[t].reshape(half_f32.shape[1:])
        for step in range(1, n_tp):
            core_sum(c, step, False).start()

    def after_core(c):
        for step in range(1, n_tp):
            core_sum(c, step, True).wait_recv()
        for at_e in range(n_expert):
            total = half_f32[c, at_e]
            rows = slice(at_e * expert_rows, (at_e + 1) * expert_rows)
            for step in range(1, n_tp):
                total = total + part_in[c, step, rows, :].astype(jnp.float32)
            half_f32[c, at_e] = total
            half_b16[c, at_e] = total.astype(jnp.bfloat16)
        for step in range(1, n_expert):
            expert_sum(c, step, False).start()

    def after_expert(c):
        for step in range(1, n_expert):
            expert_sum(c, step, True).wait_recv()
        total = half_f32[c, e]
        for step in range(1, n_expert):
            total = total + half_in[c, step].astype(jnp.float32)
        for at_a in range(n_attn):
            piece = total[at_a * batch : (at_a + 1) * batch, :]
            quad_f32[c, at_a] = piece
            quad_b16[c, at_a] = piece.astype(jnp.bfloat16)
        for step in range(1, n_attn):
            attn_sum(c, step, False).start()

    def after_attn(c):
        for step in range(1, n_attn):
            attn_sum(c, step, True).wait_recv()
        columns = slice(c * chunk, (c + 1) * chunk)
        total = quad_f32[c, a]
        for step in range(1, n_attn):
            total = total + quad_in[c, step].astype(jnp.float32)
        out_ref[:, columns] = (stream_ref[:, columns] + total).astype(out_ref.dtype)

    compute = compute_chunk_whole if total_rows <= 64 else compute_chunk
    for tick in range(chunks + 3):
        if tick < chunks:
            compute(tick)
        if 0 <= tick - 1 < chunks:
            after_core(tick - 1)
        if 0 <= tick - 2 < chunks:
            after_expert(tick - 2)
        if 0 <= tick - 3 < chunks:
            after_attn(tick - 3)

    for step in range(1, n_attn):
        attn_send(step).wait_send()

    def sends_done(back, carry):
        for step in range(1, n_expert):
            expert_copy(step, back, False).wait_send()
        for step in range(n_expert):
            for cstep in range(1, n_tp):
                core_copy(cstep, step, back, False).wait_send()
        return carry

    lax.fori_loop(0, n_attn, sends_done, 0)
    for c in range(chunks):
        for step in range(1, n_tp):
            core_sum(c, step, False).wait_send()
        for step in range(1, n_expert):
            expert_sum(c, step, False).wait_send()
        for step in range(1, n_attn):
            attn_sum(c, step, False).wait_send()


def body(
    residual,
    queries,
    new_keys,
    new_values,
    cache_keys,
    cache_values,
    lengths,
    norm_gain,
    router,
    expert_ids,
    w_gate,
    w_up,
    w_down,
):
    n_attn = lax.axis_size("attn")
    n_expert = lax.axis_size("expert")
    n_tp = lax.axis_size("tp")
    batch, width = residual.shape
    local, _, ff = w_gate.shape
    total_rows = n_attn * n_expert * n_tp * batch
    chunks = 4
    chunk = width // chunks
    tp_rows = total_rows // n_tp
    expert_rows = tp_rows // n_expert
    vmem = pl.BlockSpec(memory_space=pltpu.VMEM)
    anywhere = pl.BlockSpec(memory_space=pl.ANY)
    dma = pltpu.SemaphoreType.DMA
    bf16, f32 = jnp.bfloat16, jnp.float32
    return pl.pallas_call(
        functools.partial(kernel, (n_attn, n_expert, n_tp, chunks)),
        out_shape=jax.ShapeDtypeStruct((batch, width), bf16),
        in_specs=[vmem] * 4
        + [pl.BlockSpec(memory_space=pltpu.SMEM)]
        + [vmem] * 3
        + [anywhere] * 5,
        out_specs=vmem,
        scratch_shapes=[
            pltpu.VMEM(cache_keys.shape, bf16),
            pltpu.VMEM(cache_values.shape, bf16),
            pltpu.VMEM((local, ff, width), bf16),
            pltpu.VMEM((local, ff, width), bf16),
            pltpu.VMEM((chunks, local, ff, chunk), bf16),
            pltpu.VMEM((batch, HEADS, HEAD_DIM), f32),
            pltpu.VMEM((batch, width), f32),
            pltpu.VMEM((n_tp, n_expert, n_attn, batch, width + 256), bf16),
            pltpu.VMEM((16, width + 256), f32),
            pltpu.VMEM((total_rows, width), bf16),
            pltpu.VMEM((total_rows, 128), f32),
            pltpu.VMEM((local, total_rows, ff), bf16),
            pltpu.VMEM((n_tp, tp_rows, chunk), f32),
            pltpu.VMEM((chunks, n_tp, tp_rows, chunk), bf16),
            pltpu.VMEM((chunks, n_tp, tp_rows, chunk), bf16),
            pltpu.VMEM((chunks, n_expert, expert_rows, chunk), f32),
            pltpu.VMEM((chunks, n_expert, expert_rows, chunk), bf16),
            pltpu.VMEM((chunks, n_expert, expert_rows, chunk), bf16),
            pltpu.VMEM((chunks, n_attn, batch, chunk), f32),
            pltpu.VMEM((chunks, n_attn, batch, chunk), bf16),
            pltpu.VMEM((chunks, n_attn, batch, chunk), bf16),
            dma((2,)),
            dma((local,)),
            dma((local,)),
            dma((chunks,)),
            dma((n_attn,)),
            dma((n_attn,)),
            dma((n_expert, n_attn)),
            dma((n_expert, n_attn)),
            dma((n_tp, n_expert, n_attn)),
            dma((n_tp, n_expert, n_attn)),
            dma((chunks, n_tp)),
            dma((chunks, n_tp)),
            dma((chunks, n_expert)),
            dma((chunks, n_expert)),
            dma((chunks, n_attn)),
            dma((chunks, n_attn)),
        ],
        compiler_params=pltpu.CompilerParams(
            collective_id=0, has_side_effects=True, vmem_limit_bytes=63 * 1024 * 1024
        ),
    )(
        residual,
        queries,
        new_keys,
        new_values,
        lengths,
        norm_gain.reshape(1, width),
        router.T,
        expert_ids,
        cache_keys,
        cache_values,
        jnp.swapaxes(w_gate, 1, 2),
        jnp.swapaxes(w_up, 1, 2),
        w_down,
    )


def solution(mesh):
    rows = ("groups", "attn", "expert", "tp")
    return jax.shard_map(
        body,
        mesh=mesh,
        in_specs=(
            P(rows, None),
            P(rows, None),
            P(rows, None),
            P(rows, None),
            P(rows, None, None),
            P(rows, None, None),
            P(rows),
            P(),
            P(),
            P(rows, None),
            P("expert", None, ("attn", "tp")),
            P("expert", None, ("attn", "tp")),
            P("expert", ("attn", "tp"), None),
        ),
        out_specs=P(rows, None),
        check_vma=False,
    )
```

time: 154 us -> 56.3 us (0.37)
  waiting for transfers between devices: 84.4 us -> 0 us
  Pallas kernels: 0 us -> 54.7 us
  matrix products: 32.2 us -> 0 us
  between operations: 14.2 us -> 0.01 us
  blocking collectives: 8.83 us -> 0 us
  local copies, waits for them, and re-layouts: 8.07 us -> 1.36 us
  starting transfers between devices: 3.47 us -> 0 us
  other arithmetic: 2.42 us -> 0 us
    unnamed x3 -> x0, waiting for transfers between devices: 56.8 us -> none
    pallas_call x0 -> x1, Pallas kernels: none -> 54.7 us  [body(): pl.pallas_call(functools.partial(kernel, (n_attn, n_expert, n_tp, chunks)...]
    dot_general x9 -> x0, matrix products: 32.2 us -> none  [the longest x1 10.9 us: body(): jnp.einsum('secd,edf->secf', everything, w_gate, preferred_element_type=j...]
    all_gather x1 -> x0, waiting for transfers between devices: 23.1 us -> none  [body(): everything = lax.all_gather(received, ('attn', 'tp'), axis=0, tiled=True)]
    all_to_all x1 -> x0, blocking collectives: 8.83 us -> none  [body(): lax.all_to_all(outgoing, 'expert', split_axis=0, concat_axis=0, tiled=True)]
    all_to_all x1 -> x0, waiting for transfers between devices: 4.45 us -> none  [body(): lax.all_to_all(summed, 'expert', split_axis=0, concat_axis=0, tiled=True)]
    all_to_all x1 -> x0, starting transfers between devices: 3.42 us -> none  [body(): lax.all_to_all(summed, 'expert', split_axis=0, concat_axis=0, tiled=True)]
    reshape x6 -> x0, local copies, waits for them, and re-layouts: 2.54 us -> none  [the longest x1 0.92 us: attend_local(): query_heads = queries.reshape(row_count, KV_HEADS, group_size, HEAD_DIM)]
  transfers between devices with their start and end apart: 3 -> 0, of which waited for: 3 -> 0; matrix products, arithmetic and copies ran while one was open for 1% -> 0% of each run, Pallas kernels for 0% -> 0%
where the time goes in v1:
time: 56.3 us; the launch traced here: 56 us
  Pallas kernels  54.7 us (97%)
  local copies, waits for them, and re-layouts  1.36 us (2%)
    pallas_call x1, Pallas kernels, body(): pl.pallas_call(functools.partial(kernel, (n_attn, n_expert, n_tp, chunks)...  54.7 us
    unnamed x1, local copies, waits for them, and re-layouts  1.36 us

profile of v1, /device:TPU:0, one launch (start us, length us, event | category | flops | bytes accessed | tf_op | source)
XLA Modules:
  0.0 56.0 jit_solution(11742762248293684302)
XLA Ops:
  0.0 54.7 %shard_map.127 = bf16[4,3072]{1,0:T(4,128)(2,1)} custom-call(bf16[4,3072]{1,0:T(4,128)(2,1)} %residual_ref.1, bf16[4,3072]{1,0:T(4,128)(2,1)} %queries_ref.1, bf16[4,512]{1,0:T(4,128)(2,1)} %new_keys_ref.1, bf16[4,512]{1,0:T(4,128)(2,1)} %new_values_ref.1, s32[4]{0:T(128)} %lengths_ref.1, f32[1,3072]{1,0:T(1,128)} %bitcast.7, bf16[8,3072]{1,0:T(8,128)(2,1)} %bitcast.6, ...), custom_call_target="tpu_custom_call" | custom-call | tf_op jit(solution)/shard_map/pallas_call | solution.py:504
  54.7 1.4 %copy.15 = bf16[4,3072]{1,0:T(4,128)(2,1)} copy(bf16[4,3072]{1,0:T(4,128)(2,1)} %shard_map.127) | data formatting | bytes 49152

commit v2 on v1

--- a/solution.py
+++ b/solution.py
@@ -14,6 +14,7 @@
 TOPK = 4
 NORM_EPS = 1e-05
 MESH = pl.DeviceIdType.MESH
+PACE = (3, 1, 2, 2, 1)
 
 
 def kernel(
@@ -47,9 +48,6 @@
     part_f32,
     part_b16,
     part_in,
-    half_f32,
-    half_b16,
-    half_in,
     quad_f32,
     quad_b16,
     quad_in,
@@ -65,8 +63,6 @@
     gc_recv,
     rc_send,
     rc_recv,
-    rx_send,
-    rx_recv,
     ra_send,
     ra_recv,
 ):
@@ -81,6 +77,8 @@
     group_size = HEADS // KV_HEADS
     chunk = width // chunks
     total_rows = rows_ref.shape[0]
+    chips = n_expert * n_attn
+    chip = e * n_attn + a
 
     cache_copies = [
         pltpu.make_async_copy(keys_hbm, keys_ref, cache_sem.at[0]),
@@ -89,35 +87,56 @@
     for copy in cache_copies:
         copy.start()
 
-    def gate_copy(i):
-        return pltpu.make_async_copy(gate_hbm.at[i], gate_ref.at[i], gate_sem.at[i])
-
-    def up_copy(i):
-        return pltpu.make_async_copy(up_hbm.at[i], up_ref.at[i], up_sem.at[i])
-
-    def down_copy(c):
+    pieces = gate_sem.shape[1]
+    piece = ff // pieces
+
+    def gate_copy(i, p):
+        rows = pl.ds(p * piece, piece)
+        return pltpu.make_async_copy(
+            gate_hbm.at[i, rows], gate_ref.at[i, rows], gate_sem.at[i, p]
+        )
+
+    def up_copy(i, p):
+        rows = pl.ds(p * piece, piece)
+        return pltpu.make_async_copy(up_hbm.at[i, rows], up_ref.at[i, rows], up_sem.at[i, p])
+
+    def down_copy(c, i):
         columns = pl.ds(c * chunk, chunk)
         return pltpu.make_async_copy(
-            down_hbm.at[:, :, columns], down_ref.at[c], down_sem.at[c]
-        )
-
+            down_hbm.at[i, :, columns], down_ref.at[c, i], down_sem.at[c, i]
+        )
+
+    waiting = []
     for i in range(local):
-        gate_copy(i).start()
-        up_copy(i).start()
+        for p in range(pieces):
+            waiting.append(gate_copy(i, p))
+            waiting.append(up_copy(i, p))
     for c in range(chunks):
-        down_copy(c).start()
+        for i in range(local):
+            waiting.append(down_copy(c, i))
+
+    def start_weights(count):
+        for _ in range(min(count, len(waiting))):
+            waiting.pop(0).start()
+
+    start_weights(PACE[0])
 
     barrier = pltpu.get_barrier_semaphore()
     partners = 0
-    for axis, size, me in (("attn", n_attn, a), ("expert", n_expert, e), ("tp", n_tp, t)):
-        for step in range(1, size):
-            pl.semaphore_signal(
-                barrier,
-                inc=1,
-                device_id={axis: lax.rem(me + step, size)},
-                device_id_type=MESH,
-            )
-            partners += 1
+    for step in range(1, chips):
+        other = lax.rem(chip + step, chips)
+        pl.semaphore_signal(
+            barrier,
+            inc=1,
+            device_id={"expert": other // n_attn, "attn": lax.rem(other, n_attn)},
+            device_id_type=MESH,
+        )
+        partners += 1
+    for step in range(1, n_tp):
+        pl.semaphore_signal(
+            barrier, inc=1, device_id={"tp": lax.rem(t + step, n_tp)}, device_id_type=MESH
+        )
+        partners += 1
 
     query_f = queries_ref[...].astype(jnp.float32)
     for r in range(batch):
@@ -163,6 +182,7 @@
             attended = attended + mixed[:, k * HEAD_DIM : (k + 1) * HEAD_DIM]
         for h in range(HEADS):
             stream_ref[r : r + 1, h * HEAD_DIM : (h + 1) * HEAD_DIM] = attended[h : h + 1, :]
+        start_weights(PACE[1])
 
     stream = residual_ref[...].astype(jnp.float32) + stream_ref[...]
     stream_ref[...] = stream
@@ -255,6 +275,7 @@
             core_copy(cstep, 0, back, False).start()
 
     forward_all(0, None)
+    start_weights(PACE[2])
 
     def arrived_then_forward(back, carry):
         attn_arrived(back).wait_recv()
@@ -274,8 +295,13 @@
                 core_copy(cstep, step, back, True).wait_recv()
         return carry
 
-    lax.fori_loop(1, n_attn, arrived_then_forward, 0)
-    lax.fori_loop(0, n_attn, crossed_then_forward, 0)
+    for back in range(1, n_attn):
+        arrived_then_forward(back, 0)
+        start_weights(PACE[3])
+    for back in range(n_attn):
+        crossed_then_forward(back, 0)
+        start_weights(PACE[4])
+    start_weights(len(waiting))
     lax.fori_loop(0, n_attn, core_arrived, 0)
 
     per_stage = 16 // batch
@@ -303,8 +329,9 @@
     by_last = (((1,), (1,)), ((), ()))
 
     def first_products(i, carry):
-        gate_copy(i).wait()
-        up_copy(i).wait()
+        for p in range(pieces):
+            gate_copy(i, p).wait()
+            up_copy(i, p).wait()
 
         def one_block(b, inner):
             at = pl.ds(pl.multiple_of(b * block_rows, block_rows), block_rows)
@@ -337,34 +364,23 @@
             device_id_type=MESH,
         )
 
-    def expert_sum(c, step, reverse):
-        other = lax.rem(e + n_expert - step, n_expert) if reverse else lax.rem(e + step, n_expert)
-        return pltpu.make_async_remote_copy(
-            src_ref=half_b16.at[c, other],
-            dst_ref=half_in.at[c, step],
-            send_sem=rx_send.at[c, step],
-            recv_sem=rx_recv.at[c, step],
-            device_id={"expert": other},
-            device_id_type=MESH,
-        )
-
-    def attn_sum(c, step, reverse):
-        other = lax.rem(a + n_attn - step, n_attn) if reverse else lax.rem(a + step, n_attn)
+    def chip_sum(c, step, reverse):
+        other = lax.rem(chip + chips - step, chips) if reverse else lax.rem(chip + step, chips)
         return pltpu.make_async_remote_copy(
             src_ref=quad_b16.at[c, other],
             dst_ref=quad_in.at[c, step],
             send_sem=ra_send.at[c, step],
             recv_sem=ra_recv.at[c, step],
-            device_id={"attn": other},
+            device_id={"expert": other // n_attn, "attn": lax.rem(other, n_attn)},
             device_id_type=MESH,
         )
 
     tp_rows = total_rows // n_tp
-    expert_rows = tp_rows // n_expert
     tp_block = min(tp_rows, 32)
 
     def compute_chunk(c):
-        down_copy(c).wait()
+        for i in range(local):
+            down_copy(c, i).wait()
         for at_t in range(n_tp):
 
             def one_block(b, inner, at_t=at_t):
@@ -378,78 +394,70 @@
                         down_ref[c, i],
                         preferred_element_type=jnp.float32,
                     )
-                part_f32[at_t, at, :] = total
+                part_f32[c, at_t, at, :] = total
                 part_b16[c, at_t, at, :] = total.astype(jnp.bfloat16)
                 return inner
 
-            if tp_rows > tp_block:
-                lax.fori_loop(0, tp_rows // tp_block, one_block, 0)
-            else:
-                one_block(0, 0)
-        half_f32[c] = part_f32[t].reshape(half_f32.shape[1:])
+            lax.fori_loop(0, tp_rows // tp_block, one_block, 0)
         for step in range(1, n_tp):
             core_sum(c, step, False).start()
 
     def compute_chunk_whole(c):
-        down_copy(c).wait()
+        for i in range(local):
+            down_copy(c, i).wait()
         total = jnp.dot(hidden_ref[0], down_ref[c, 0], preferred_element_type=jnp.float32)
         for i in range(1, local):
             total = total + jnp.dot(
                 hidden_ref[i], down_ref[c, i], preferred_element_type=jnp.float32
             )
         for at_t in range(n_tp):
-            piece = total[at_t * tp_rows : (at_t + 1) * tp_rows, :]
-            part_f32[at_t] = piece
-            part_b16[c, at_t] = piece.astype(jnp.bfloat16)
-        half_f32[c] = part_f32[t].reshape(half_f32.shape[1:])
+            rows = total[at_t * tp_rows : (at_t + 1) * tp_rows, :]
+            part_f32[c, at_t] = rows
+            part_b16[c, at_t] = rows.astype(jnp.bfloat16)
         for step in range(1, n_tp):
             core_sum(c, step, False).start()
 
-    def after_core(c):
+    def send_chunk(c):
         for step in range(1, n_tp):
             core_sum(c, step, True).wait_recv()
-        for at_e in range(n_expert):
-            total = half_f32[c, at_e]
-            rows = slice(at_e * expert_rows, (at_e + 1) * expert_rows)
+
+        def one_block(b, carry):
+            at = pl.ds(pl.multiple_of(b * 16, 16), 16)
+            total = part_f32[c, t, at, :]
             for step in range(1, n_tp):
-                total = total + part_in[c, step, rows, :].astype(jnp.float32)
-            half_f32[c, at_e] = total
-            half_b16[c, at_e] = total.astype(jnp.bfloat16)
-        for step in range(1, n_expert):
-            expert_sum(c, step, False).start()
-
-    def after_expert(c):
-        for step in range(1, n_expert):
-            expert_sum(c, step, True).wait_recv()
-        total = half_f32[c, e]
-        for step in range(1, n_expert):
-            total = total + half_in[c, step].astype(jnp.float32)
-        for at_a in range(n_attn):
-            piece = total[at_a * batch : (at_a + 1) * batch, :]
-            quad_f32[c, at_a] = piece
-            quad_b16[c, at_a] = piece.astype(jnp.bfloat16)
-        for step in range(1, n_attn):
-            attn_sum(c, step, False).start()
-
-    def after_attn(c):
-        for step in range(1, n_attn):
-            attn_sum(c, step, True).wait_recv()
+                total = total + part_in[c, step, at, :].astype(jnp.float32)
+            for j in range(per_stage):
+                rows = total[j * batch : (j + 1) * batch, :]
+                quad_f32[c, b * per_stage + j] = rows
+                quad_b16[c, b * per_stage + j] = rows.astype(jnp.bfloat16)
+            return carry
+
+        lax.fori_loop(0, tp_rows // 16, one_block, 0)
+
+        def one_send(step, carry):
+            chip_sum(c, step, False).start()
+            return carry
+
+        lax.fori_loop(1, chips, one_send, 0)
+
+    def finish_chunk(c):
         columns = slice(c * chunk, (c + 1) * chunk)
-        total = quad_f32[c, a]
-        for step in range(1, n_attn):
-            total = total + quad_in[c, step].astype(jnp.float32)
-        out_ref[:, columns] = (stream_ref[:, columns] + total).astype(out_ref.dtype)
+
+        def one_arrival(step, total):
+            chip_sum(c, step, True).wait_recv()
+            return total + quad_in[c, step].astype(jnp.float32)
+
+        total = lax.fori_loop(1, chips, one_arrival, stream_ref[:, columns] + quad_f32[c, chip])
+        out_ref[:, columns] = total.astype(out_ref.dtype)
 
     compute = compute_chunk_whole if total_rows <= 64 else compute_chunk
-    for tick in range(chunks + 3):
-        if tick < chunks:
-            compute(tick)
-        if 0 <= tick - 1 < chunks:
-            after_core(tick - 1)
-        if 0 <= tick - 2 < chunks:
-            after_expert(tick - 2)
-        if 0 <= tick - 3 < chunks:
-            after_attn(tick - 3)
+    for c in range(chunks):
+        compute(c)
+        if c > 0:
+            send_chunk(c - 1)
+    send_chunk(chunks - 1)
+    for c in range(chunks):
+        finish_chunk(c)
 
     for step in range(1, n_attn):
         attn_send(step).wait_send()
@@ -466,10 +474,12 @@
     for c in range(chunks):
         for step in range(1, n_tp):
             core_sum(c, step, False).wait_send()
-        for step in range(1, n_expert):
-            expert_sum(c, step, False).wait_send()
-        for step in range(1, n_attn):
-            attn_sum(c, step, False).wait_send()
+
+        def one_left(step, carry, c=c):
+            chip_sum(c, step, False).wait_send()
+            return carry
+
+        lax.fori_loop(1, chips, one_left, 0)
 
 
 def body(
@@ -493,10 +503,11 @@
     batch, width = residual.shape
     local, _, ff = w_gate.shape
     total_rows = n_attn * n_expert * n_tp * batch
-    chunks = 4
+    chunks = 2
     chunk = width // chunks
     tp_rows = total_rows // n_tp
-    expert_rows = tp_rows // n_expert
+    chips = n_expert * n_attn
+    pieces = 2 if ff % 32 == 0 else 1
     vmem = pl.BlockSpec(memory_space=pltpu.VMEM)
     anywhere = pl.BlockSpec(memory_space=pl.ANY)
     dma = pltpu.SemaphoreType.DMA
@@ -522,19 +533,16 @@
             pltpu.VMEM((total_rows, width), bf16),
             pltpu.VMEM((total_rows, 128), f32),
             pltpu.VMEM((local, total_rows, ff), bf16),
-            pltpu.VMEM((n_tp, tp_rows, chunk), f32),
+            pltpu.VMEM((chunks, n_tp, tp_rows, chunk), f32),
             pltpu.VMEM((chunks, n_tp, tp_rows, chunk), bf16),
             pltpu.VMEM((chunks, n_tp, tp_rows, chunk), bf16),
-            pltpu.VMEM((chunks, n_expert, expert_rows, chunk), f32),
-            pltpu.VMEM((chunks, n_expert, expert_rows, chunk), bf16),
-            pltpu.VMEM((chunks, n_expert, expert_rows, chunk), bf16),
-            pltpu.VMEM((chunks, n_attn, batch, chunk), f32),
-            pltpu.VMEM((chunks, n_attn, batch, chunk), bf16),
-            pltpu.VMEM((chunks, n_attn, batch, chunk), bf16),
+            pltpu.VMEM((chunks, chips, batch, chunk), f32),
+            pltpu.VMEM((chunks, chips, batch, chunk), bf16),
+            pltpu.VMEM((chunks, chips, batch, chunk), bf16),
             dma((2,)),
-            dma((local,)),
-            dma((local,)),
-            dma((chunks,)),
+            dma((local, pieces)),
+            dma((local, pieces)),
+            dma((chunks, local)),
             dma((n_attn,)),
             dma((n_attn,)),
             dma((n_expert, n_attn)),
@@ -543,10 +551,8 @@
             dma((n_tp, n_expert, n_attn)),
             dma((chunks, n_tp)),
             dma((chunks, n_tp)),
-            dma((chunks, n_expert)),
-            dma((chunks, n_expert)),
-            dma((chunks, n_attn)),
-            dma((chunks, n_attn)),
+            dma((chunks, chips)),
+            dma((chunks, chips)),
         ],
         compiler_params=pltpu.CompilerParams(
             collective_id=0, has_side_effects=True, vmem_limit_bytes=63 * 1024 * 1024

time: 56.3 us -> 39.7 us (0.71)
  Pallas kernels: 54.7 us -> 38.1 us
    pallas_call x1, Pallas kernels: 54.7 us -> 38.1 us  [body(): pl.pallas_call(functools.partial(kernel, (n_attn, n_expert, n_tp, chunks)...]
where the time goes in v2:
time: 39.7 us; the launch traced here: 39.5 us
  Pallas kernels  38.1 us (96%)
  local copies, waits for them, and re-layouts  1.36 us (3%)
    pallas_call x1, Pallas kernels, body(): pl.pallas_call(functools.partial(kernel, (n_attn, n_expert, n_tp, chunks)...  38.1 us
    unnamed x1, local copies, waits for them, and re-layouts  1.36 us

profile of v2, /device:TPU:0, one launch (start us, length us, event | category | flops | bytes accessed | tf_op | source)
XLA Modules:
  0.0 39.5 jit_solution(9119081234694648205)
XLA Ops:
  0.0 38.1 %shard_map.127 = bf16[4,3072]{1,0:T(4,128)(2,1)} custom-call(bf16[4,3072]{1,0:T(4,128)(2,1)} %residual_ref.1, bf16[4,3072]{1,0:T(4,128)(2,1)} %queries_ref.1, bf16[4,512]{1,0:T(4,128)(2,1)} %new_keys_ref.1, bf16[4,512]{1,0:T(4,128)(2,1)} %new_values_ref.1, s32[4]{0:T(128)} %lengths_ref.1, f32[1,3072]{1,0:T(1,128)} %bitcast.7, bf16[8,3072]{1,0:T(8,128)(2,1)} %bitcast.6, ...), custom_call_target="tpu_custom_call" | custom-call | tf_op jit(solution)/shard_map/pallas_call | solution.py:515
  38.1 1.4 %copy.15 = bf16[4,3072]{1,0:T(4,128)(2,1)} copy(bf16[4,3072]{1,0:T(4,128)(2,1)} %shard_map.127) | data formatting | bytes 49152

commit v3 on v2

--- a/solution.py
+++ b/solution.py
@@ -14,7 +14,7 @@
 TOPK = 4
 NORM_EPS = 1e-05
 MESH = pl.DeviceIdType.MESH
-PACE = (3, 1, 2, 2, 1)
+PACE = (3, 1, 1, 3, 2)
 
 
 def kernel(
@@ -151,38 +151,49 @@
     new_keys = new_keys_ref[...].astype(jnp.float32)
     new_values = new_values_ref[...].astype(jnp.float32)
     score_scale = HEAD_DIM ** (-0.5)
-    for copy in cache_copies:
-        copy.wait()
+    blocks = [
+        jnp.where(own_kv, jnp.concatenate([query_rows[r]] * KV_HEADS, axis=1), 0.0)
+        for r in range(batch)
+    ]
+    own_score = jnp.concatenate(
+        [
+            jnp.sum(blocks[r] * new_keys[r : r + 1, :], axis=1, keepdims=True)
+            for r in range(batch)
+        ],
+        axis=0,
+    )
+    own_score = own_score * score_scale
+    cache_copies[0].wait()
+    scores = []
     for r in range(batch):
-        query = query_rows[r]
-        blocks = jnp.where(own_kv, jnp.concatenate([query] * KV_HEADS, axis=1), 0.0)
-        scores = (
-            lax.dot_general(
-                blocks.astype(jnp.bfloat16),
-                keys_ref[r],
-                (((1,), (1,)), ((), ())),
-                preferred_element_type=jnp.float32,
-            )
-            * score_scale
-        )
-        scores = jnp.where(position < lengths_ref[r], scores, -jnp.inf)
-        own_score = (
-            jnp.sum(blocks * new_keys[r : r + 1, :], axis=1, keepdims=True) * score_scale
-        )
-        highest = jnp.maximum(jnp.max(scores, axis=1, keepdims=True), own_score)
-        weights = jnp.exp(scores - highest)
-        own_weight = jnp.exp(own_score - highest)
-        denominator = jnp.sum(weights, axis=1, keepdims=True) + own_weight
-        probabilities = (weights / denominator).astype(jnp.bfloat16)
-        own_prob = (own_weight / denominator).astype(jnp.bfloat16).astype(jnp.float32)
-        mixed = jnp.dot(probabilities, values_ref[r], preferred_element_type=jnp.float32)
-        mixed = jnp.where(own_kv, mixed + own_prob * new_values[r : r + 1, :], 0.0)
+        product = lax.dot_general(
+            blocks[r].astype(jnp.bfloat16),
+            keys_ref[r],
+            (((1,), (1,)), ((), ())),
+            preferred_element_type=jnp.float32,
+        )
+        scores.append(jnp.where(position < lengths_ref[r], product * score_scale, -jnp.inf))
+    scores = jnp.concatenate(scores, axis=0)
+    start_weights(PACE[1])
+    highest = jnp.maximum(jnp.max(scores, axis=1, keepdims=True), own_score)
+    weights = jnp.exp(scores - highest)
+    own_weight = jnp.exp(own_score - highest)
+    denominator = jnp.sum(weights, axis=1, keepdims=True) + own_weight
+    probabilities = (weights / denominator).astype(jnp.bfloat16)
+    own_prob = (own_weight / denominator).astype(jnp.bfloat16).astype(jnp.float32)
+    cache_copies[1].wait()
+    for r in range(batch):
+        of_request = slice(r * HEADS, (r + 1) * HEADS)
+        mixed = jnp.dot(
+            probabilities[of_request], values_ref[r], preferred_element_type=jnp.float32
+        )
+        mixed = mixed + own_prob[of_request] * new_values[r : r + 1, :]
+        mixed = jnp.where(own_kv, mixed, 0.0)
         attended = mixed[:, :HEAD_DIM]
         for k in range(1, KV_HEADS):
             attended = attended + mixed[:, k * HEAD_DIM : (k + 1) * HEAD_DIM]
         for h in range(HEADS):
             stream_ref[r : r + 1, h * HEAD_DIM : (h + 1) * HEAD_DIM] = attended[h : h + 1, :]
-        start_weights(PACE[1])
 
     stream = residual_ref[...].astype(jnp.float32) + stream_ref[...]
     stream_ref[...] = stream
@@ -336,11 +347,11 @@
         def one_block(b, inner):
             at = pl.ds(pl.multiple_of(b * block_rows, block_rows), block_rows)
             gate_act = lax.dot_general(
-                rows_ref[at, :], gate_ref[i], by_last, preferred_element_type=jnp.float32
-            )
+                gate_ref[i], rows_ref[at, :], by_last, preferred_element_type=jnp.float32
+            ).T
             up_act = lax.dot_general(
-                rows_ref[at, :], up_ref[i], by_last, preferred_element_type=jnp.float32
-            )
+                up_ref[i], rows_ref[at, :], by_last, preferred_element_type=jnp.float32
+            ).T
             valid = lane < EXPERTS
             chosen = jnp.where((lane == e * local + i) & valid, weights_ref[at, :], 0.0)
             scale = jnp.sum(chosen, axis=1, keepdims=True)

time: 39.7 us -> 37.5 us (0.945)
  Pallas kernels: 38.1 us -> 35.9 us
    pallas_call x1, Pallas kernels: 38.1 us -> 35.9 us  [body(): pl.pallas_call(functools.partial(kernel, (n_attn, n_expert, n_tp, chunks)...]
where the time goes in v3:
time: 37.5 us; the launch traced here: 37.2 us
  Pallas kernels  35.9 us (96%)
  local copies, waits for them, and re-layouts  1.36 us (4%)
    pallas_call x1, Pallas kernels, body(): pl.pallas_call(functools.partial(kernel, (n_attn, n_expert, n_tp, chunks)...  35.9 us
    unnamed x1, local copies, waits for them, and re-layouts  1.36 us

profile of v3, /device:TPU:0, one launch (start us, length us, event | category | flops | bytes accessed | tf_op | source)
XLA Modules:
  0.0 37.2 jit_solution(18381401437880454959)
XLA Ops:
  0.0 35.9 %shard_map.127 = bf16[4,3072]{1,0:T(4,128)(2,1)} custom-call(bf16[4,3072]{1,0:T(4,128)(2,1)} %residual_ref.1, bf16[4,3072]{1,0:T(4,128)(2,1)} %queries_ref.1, bf16[4,512]{1,0:T(4,128)(2,1)} %new_keys_ref.1, bf16[4,512]{1,0:T(4,128)(2,1)} %new_values_ref.1, s32[4]{0:T(128)} %lengths_ref.1, f32[1,3072]{1,0:T(1,128)} %bitcast.7, bf16[8,3072]{1,0:T(8,128)(2,1)} %bitcast.6, ...), custom_call_target="tpu_custom_call" | custom-call | tf_op jit(solution)/shard_map/pallas_call | solution.py:526
  35.9 1.4 %copy.15 = bf16[4,3072]{1,0:T(4,128)(2,1)} copy(bf16[4,3072]{1,0:T(4,128)(2,1)} %shard_map.127) | data formatting | bytes 49152
